TPU v7x, 32 devices: a whole 2x2x4 slice. The times are simulated.
32 devices in a mesh: grp: 2 (over y), rec: 4 (over z), smp: 4 (over x, core).
Axes of the slice: x: 2, y: 2, z: 4, core: 2. Of those that a mesh axis runs over, the one named last changes fastest.
Arguments:
- records: bfloat16 [2048, 16384], P(('grp', 'rec'), 'smp'), parts along dimension 0, may hold values from -24 to 24
- start_modes: float32 [4, 8192, 128], P('smp', ('grp', 'rec')), parts along dimension 1, may hold values from -6 to 6
Outputs:
- covariance: float32 [4, 8192, 16384], P(None, ('grp', 'rec'), 'smp'), parts along dimension 1
- modes: float32 [4, 8192, 128], P('smp', ('grp', 'rec')), parts along dimension 1
- projections: float32 [2048, 128], P(('grp', 'rec')), parts along dimension 0
There are 2 independent parts, one for each index of `grp`. A program takes and returns all parts, laid end to end along the dimension named above; each array names one. Nothing has to cross between parts.
All inputs are finite; a program needn't handle non-finite values.
Results may differ from a plain program's by a relative error of at most 0.0003.
Values may be sent and summed in bfloat16 or wider, within the bound.
A program may use at most 192 MiB of HBM per device.

v0:
```python
import math

import jax
import jax.numpy as jnp
from jax import lax
from jax.sharding import PartitionSpec as P

ITERS = 2


def factor_apply(block, inner):
    factor = jnp.linalg.cholesky(inner)
    return lax.linalg.triangular_solve(factor, block, left_side=False, lower=True, transpose_a=True)


def on_device(records, start_modes):
    rec_dev, width = records.shape
    panels = lax.axis_size("smp")
    full_width = width * panels
    columns = lax.all_to_all(records, "rec", split_axis=1, concat_axis=0, tiled=True)
    total, sub_width = columns.shape
    row_block = lax.all_gather(columns, "smp", axis=1, tiled=True)
    tile = (
        lax.dot_general(
            row_block,
            lax.all_gather(records, "rec", axis=0, tiled=True),
            (((0,), (0,)), ((), ())),
            preferred_element_type=jnp.float32,
        )
        / total
    )
    covariance = tile.reshape(panels, sub_width, width)
    kept = start_modes.shape[2]
    subspace = start_modes.reshape(sub_width, kept)
    for step in range(ITERS):
        partial_value = jnp.dot(
            tile,
            lax.all_gather(subspace, "rec", axis=0, tiled=True),
            precision=lax.Precision.HIGHEST,
        )
        subspace = lax.psum_scatter(partial_value, "smp", scatter_dimension=0, tiled=True)
    inner = lax.psum(jnp.dot(subspace.T, subspace, precision=lax.Precision.HIGHEST), ("rec", "smp"))
    subspace = factor_apply(subspace, inner)
    records_wide = records.astype(jnp.float32)
    partial_amp = jnp.dot(
        records_wide,
        lax.all_gather(subspace, "rec", axis=0, tiled=True),
        precision=lax.Precision.HIGHEST,
    )
    amplitude = lax.psum(partial_amp, "smp") / math.sqrt(full_width)
    modes = (subspace * math.sqrt(full_width)).reshape(1, sub_width, kept)
    return (covariance, modes, amplitude)


def solution(mesh):
    in_specs = (P(("grp", "rec"), "smp"), P("smp", ("grp", "rec"), None))
    out_specs = (
        P(None, ("grp", "rec"), "smp"),
        P("smp", ("grp", "rec"), None),
        P(("grp", "rec"), None),
    )
    return jax.shard_map(
        on_device, mesh=mesh, in_specs=in_specs, out_specs=out_specs, check_vma=False
    )
```

profile of v0, /device:TPU:0, one launch (start us, length us, event | category | flops | bytes accessed | tf_op | source)
XLA Modules:
  0.0 740.1 jit_solution(13675355471693773370)
XLA Ops:
  7.2 0.0 all-gather.9.cloned.1.call-start
  7.2 0.7 all-gather.9.cloned.1.call-update
  7.9 0.0 all-gather.7.cloned.1.call-start
  8.0 0.8 copy-done
  8.8 2.4 copy.11
  11.2 109.2 %all_to_all.19 = bf16[256,4,1024]{0,2,1:T(8,128)(2,1)} all-to-all(bf16[256,4,1024]{0,2,1:T(8,128)(2,1)} %bitcast.32), channel_id=1, replica_groups=mesh['grp'=2,'rec'=4,'smp'=4] {'rec'}, dimensions={1} | all-to-all | bytes 4194304 | tf_op jit(solution)/shard_map/all_to_all | solution.py:20
  120.4 3.9 copy.12
  124.4 0.0 all-gather.7.cloned.1.call-update
  124.4 0.0 all-gather.15.cloned.1.call-start
  124.4 0.7 all-gather.15.cloned.1.call-update
  125.1 0.0 reduce-scatter.3.cloned.1.call-start
  125.2 75.8 %all-gather.9.cloned.1.call-done = bf16[1024,4096]{1,0:T(8,128)(2,1)} async-done(((bf16[256,4096]{1,0:T(8,128)(2,1)}), bf16[1024,4096]{1,0:T(8,128)(2,1)}) %all-gather.9.cloned.1.call-update) | async-done | bytes 8388624 | tf_op jit(solution)/shard_map/all_gather | solution.py:26
  201.0 59.6 %all-gather.7.cloned.1.call-done = bf16[1024,4096]{1,0:T(8,128)(2,1)} async-done(((bf16[1024,1024]{1,0:T(8,128)(2,1)}), bf16[1024,4096]{1,0:T(8,128)(2,1)}) %all-gather.7.cloned.1.call-update) | async-done | bytes 8388624 | tf_op jit(solution)/shard_map/all_gather | solution.py:22
  260.6 46.3 %convolution_multiply_fusion = f32[4096,4096]{1,0:T(8,128)} fusion(bf16[1024,4096]{1,0:T(8,128)(2,1)} %all-gather.7.cloned.1.call-done, bf16[1024,4096]{1,0:T(8,128)(2,1)} %all-gather.9.cloned.1.call-done), kind=kOutput, calls=%fused_computation | convolution fusion | flops 34376515584 | bytes 83886080 | tf_op jit(solution)/shard_map/dot_general | solution.py:24
  306.9 1.3 all-gather.15.cloned.1.call-done
  308.2 59.0 %fusion = f32[4096,128]{1,0:T(8,128)} fusion(f32[4096,4096]{1,0:T(8,128)} %convolution_multiply_fusion, f32[1,4096,128]{2,1,0:T(8,128)} %all-gather.15.cloned.1.call-done), kind=kOutput, calls=%fused_computation.1 | convolution fusion | flops 25769803776 | bytes 71303168 | tf_op jit(solution)/shard_map/dot_general | solution.py:36
  367.1 0.0 reduce-scatter.3.cloned.1.call-update
  367.2 0.0 all-gather.11.cloned.1.call-start
  367.2 30.3 %reduce-scatter.3.cloned.1.call-done = f32[1024,128]{1,0:T(8,128)} async-done(((f32[4096,128]{1,0:T(8,128)}), f32[1024,128]{1,0:T(8,128)}) %reduce-scatter.3.cloned.1.call-update) | async-done | bytes 524304 | tf_op jit(solution)/shard_map/reduce_scatter | solution.py:41
  397.5 0.0 all-gather.11.cloned.1.call-update
  397.5 0.0 reduce-scatter.5.cloned.1.call-start
  397.6 47.4 %all-gather.11.cloned.1.call-done = f32[4096,128]{1,0:T(8,128)} async-done(((f32[1024,128]{1,0:T(8,128)}), f32[4096,128]{1,0:T(8,128)}) %all-gather.11.cloned.1.call-update) | async-done | bytes 2097168 | tf_op jit(solution)/shard_map/all_gather | solution.py:38
  444.9 59.0 %fusion.6 = f32[4096,128]{1,0:T(8,128)} fusion(f32[4096,4096]{1,0:T(8,128)} %convolution_multiply_fusion, f32[4096,128]{1,0:T(8,128)} %all-gather.11.cloned.1.call-done), kind=kOutput, calls=%fused_computation.16 | convolution fusion | flops 25769803776 | bytes 71303168 | tf_op jit(solution)/shard_map/dot_general | solution.py:36
  503.9 0.0 reduce-scatter.5.cloned.1.call-update
  503.9 0.0 all-reduce.3.cloned.1.call-start
  504.0 30.3 %reduce-scatter.5.cloned.1.call-done = f32[1024,128]{1,0:T(8,128)} async-done(((f32[4096,128]{1,0:T(8,128)}), f32[1024,128]{1,0:T(8,128)}) %reduce-scatter.5.cloned.1.call-update) | async-done | bytes 524304 | tf_op jit(solution)/shard_map/reduce_scatter | solution.py:41
  534.3 2.8 fusion.7
  537.1 0.0 all-reduce.3.cloned.1.call-update
  537.1 0.3 all-gather.13.cloned.1.call-start
  537.4 85.4 %all-reduce.3.cloned.1.call-done = f32[128,128]{0,1:T(8,128)} async-done(((f32[128,128]{0,1:T(8,128)}), f32[128,128]{0,1:T(8,128)}) %all-reduce.3.cloned.1.call-update) | async-done | bytes 65552 | tf_op jit(solution)/shard_map/psum | solution.py:42
  622.8 0.9 copy.14
  623.7 0.9 fusion.5
  624.6 11.7 %cholesky.16 = f32[128,128]{1,0:T(8,128)S(1)} custom-call(f32[128,128]{1,0:T(8,128)S(1)} %fusion.5), custom_call_target="Cholesky" | custom-call | tf_op jit(solution)/shard_map/jit(cholesky)/cholesky | solution.py:12
  636.3 0.6 compare_reduce_fusion
  637.0 0.7 fusion.2
  637.6 9.8 %custom-call.6 = f32[1,128,128]{1,2,0:T(8,128)S(1)} custom-call(f32[1,128,128]{2,1,0:T(8,128)S(1)} %fusion.2), custom_call_target="InvertDiagBlocksLowerTriangular" | custom-call | tf_op jit(solution)/shard_map/triangular_solve | solution.py:13
  647.4 2.4 fusion.3
  649.9 0.0 all-gather.13.cloned.1.call-update
  649.9 0.0 copy-start.1
  649.9 0.0 all-reduce.5.cloned.1.call-start
  649.9 47.6 %all-gather.13.cloned.1.call-done = f32[4096,128]{1,0:T(8,128)} async-done(((f32[1024,128]{1,0:T(8,128)}), f32[4096,128]{1,0:T(8,128)}) %all-gather.13.cloned.1.call-update) | async-done | bytes 2097168 | tf_op jit(solution)/shard_map/all_gather | solution.py:47
  697.5 4.1 convolution_bitcast_fusion
  701.6 0.0 all-reduce.5.cloned.1.call-update
  701.6 0.0 copy-done.1
  701.6 0.8 multiply_bitcast_fusion
  702.5 29.4 %all-reduce.5.cloned.1.call-done = f32[256,128]{0,1:T(8,128)} async-done(((f32[256,128]{0,1:T(8,128)}), f32[256,128]{0,1:T(8,128)}) %all-reduce.5.cloned.1.call-update) | async-done | bytes 131088 | tf_op jit(solution)/shard_map/psum | solution.py:50
  731.9 0.9 broadcast_multiply_fusion
  732.8 0.8 copy.15
  (2 shorter events, 0.0 us)
Async XLA Ops:
  7.2 1.6 copy-start
  7.2 193.8 %all-gather.9.cloned.1.call-start = ((), (), s32[]{:S(2)}) async-start(), calls=%async_computation.4 | async-start | bytes 10485760 | tf_op jit(solution)/shard_map/all_gather | solution.py:26
  7.9 252.7 %all-gather.7.cloned.1.call-start = ((), (), s32[]{:S(2)}) async-start(), calls=%async_computation.3 | async-start | bytes 10485760 | tf_op jit(solution)/shard_map/all_gather | solution.py:22
  124.4 183.8 %all-gather.15.cloned.1.call-start = ((), (), s32[]{:S(2)}) async-start(), calls=%async_computation.11 | async-start | bytes 2621440 | tf_op jit(solution)/shard_map/all_gather | solution.py:38
  125.1 272.4 %reduce-scatter.3.cloned.1.call-start = ((), (), s32[]{:S(2)}) async-start(), calls=%async_computation.5 | async-start | bytes 2621440 | tf_op jit(solution)/shard_map/reduce_scatter | solution.py:41
  367.2 77.8 %all-gather.11.cloned.1.call-start = ((), (), s32[]{:S(2)}) async-start(), calls=%async_computation.6 | async-start | bytes 2621440 | tf_op jit(solution)/shard_map/all_gather | solution.py:38
  397.5 136.8 %reduce-scatter.5.cloned.1.call-start = ((), (), s32[]{:S(2)}) async-start(), calls=%async_computation.7 | async-start | bytes 2621440 | tf_op jit(solution)/shard_map/reduce_scatter | solution.py:41
  503.9 118.9 %all-reduce.3.cloned.1.call-start = ((), (), s32[]{:S(2)}) async-start(), calls=%async_computation.8 | async-start | bytes 131072 | tf_op jit(solution)/shard_map/psum | solution.py:42
  537.1 160.4 %all-gather.13.cloned.1.call-start = ((), (), s32[]{:S(2)}) async-start(), calls=%async_computation.9 | async-start | bytes 2621440 | tf_op jit(solution)/shard_map/all_gather | solution.py:47
  649.9 51.7 %copy-start.1 = (f32[1024,128]{1,0:T(8,128)S(1)}, f32[1024,128]{1,0:T(8,128)}, u32[]{:S(2)}) copy-start(f32[1024,128]{1,0:T(8,128)} %fusion.3) | copy-start | bytes 1572868
  649.9 82.0 %all-reduce.5.cloned.1.call-start = ((), (), s32[]{:S(2)}) async-start(), calls=%async_computation.10 | async-start | bytes 262144 | tf_op jit(solution)/shard_map/psum | solution.py:50
Sparse Core Ops, SparseCore 0:
  9.6 191.3 all-gather.8
  203.1 57.4 all-gather.6
  262.2 45.9 all-gather.14
  367.3 30.1 reduce-scatter.2
  399.0 45.9 all-gather.10
  504.1 30.1 reduce-scatter.4
  538.3 84.4 all-reduce.2
  650.0 47.4 all-gather.12
  701.7 30.1 all-reduce.4
where the time goes:
time: 741 us; the launch traced here: 740 us
  waiting for transfers between devices  409 us (55%)
  matrix products  173 us (23%)
  blocking collectives  109 us (15%)
  other arithmetic  25.5 us (3%)
  between operations  13.9 us (2%)
  local copies, waits for them, and re-layouts  8.86 us (1%)
    dot_general x2, matrix products, on_device(): jnp.dot(tile, lax.all_gather(subspace, 'rec', axis=0, tiled=True), precis...  118 us
    all_to_all x1, blocking collectives, on_device(): lax.all_to_all(records, 'rec', split_axis=1, concat_axis=0, tiled=True)  109 us
    all_gather x3, waiting for transfers between devices, on_device(): lax.all_gather(subspace, 'rec', axis=0, tiled=True)  96.3 us
    psum x1, waiting for transfers between devices, on_device(): lax.psum(jnp.dot(subspace.T, subspace, precision=lax.Precision.HIGHEST),...  85.4 us
    all_gather x1, waiting for transfers between devices, on_device(): lax.all_gather(records, 'rec', axis=0, tiled=True)  75.8 us
    reduce_scatter x2, waiting for transfers between devices, on_device(): lax.psum_scatter(partial_value, 'smp', scatter_dimension=0, tiled=True)  60.5 us
    all_gather x1, waiting for transfers between devices, on_device(): row_block = lax.all_gather(columns, 'smp', axis=1, tiled=True)  59.6 us
    dot_general x1, matrix products, on_device(): lax.dot_general(row_block, lax.all_gather(records, 'rec', axis=0, tiled=T...  46.3 us
  transfers between devices with their start and end apart: 9, of which 9 were waited for; matrix products, arithmetic and copies ran while one was open for 7% of the time, Pallas kernels for 0%

commit v1 on v0

v1 whole, which is shorter than its diff:
```python
import math

import jax
import jax.numpy as jnp
from jax import lax
from jax.sharding import PartitionSpec as P

HIGHEST = lax.Precision.HIGHEST


def pieces(block):
    parts = []
    for _ in range(2):
        high = lax.reduce_precision(block, 8, 7)
        parts.append(high.astype(jnp.bfloat16))
        block = block - high
    parts.append(block.astype(jnp.bfloat16))
    return jnp.concatenate(parts, axis=1)


def exact_dot(left, block, contract):
    kept = block.shape[1]
    out = lax.dot_general(
        left, pieces(block), (((contract,), (0,)), ((), ())), preferred_element_type=jnp.float32
    )
    return out[:, :kept] + out[:, kept : 2 * kept] + out[:, 2 * kept :]


def on_device(records, start_modes):
    rec_dev, width = records.shape
    panels = lax.axis_size("smp")
    total = rec_dev * lax.axis_size("rec")
    sub_width, kept = start_modes.shape[1:]
    full_width = width * panels
    at = lax.axis_index("rec")

    block = lax.all_gather(records, "rec", axis=0, tiled=True)
    own = lax.dynamic_slice_in_dim(block, at * sub_width, sub_width, axis=1)
    row_block = lax.all_gather(own, "smp", axis=1, tiled=True)

    gram = lax.psum(
        lax.dot_general(
            records, block, (((1,), (1,)), ((), ())), preferred_element_type=jnp.float32
        ),
        "smp",
    ) / total
    first = lax.psum(exact_dot(own, start_modes[0], 1), ("rec", "smp"))
    second_own = jnp.dot(gram, first, precision=HIGHEST)
    second = lax.all_gather(second_own, "rec", axis=0, tiled=True)
    amplitude = jnp.dot(gram, second, precision=HIGHEST)
    inner = lax.psum(jnp.dot(second_own.T, amplitude, precision=HIGHEST), "rec") / total

    tile = (
        lax.dot_general(
            row_block, block, (((0,), (0,)), ((), ())), preferred_element_type=jnp.float32
        )
        / total
    )
    covariance = tile.reshape(panels, sub_width, width)

    factor = jnp.linalg.cholesky(inner)
    solved = lax.linalg.triangular_solve(
        factor,
        jnp.concatenate([second, amplitude], axis=0),
        left_side=False,
        lower=True,
        transpose_a=True,
    )
    modes = exact_dot(own, solved[:total], 0) * (math.sqrt(full_width) / total)
    projections = solved[total:] / math.sqrt(full_width)
    return (covariance, modes.reshape(1, sub_width, kept), projections)


def solution(mesh):
    in_specs = (P(("grp", "rec"), "smp"), P("smp", ("grp", "rec"), None))
    out_specs = (
        P(None, ("grp", "rec"), "smp"),
        P("smp", ("grp", "rec"), None),
        P(("grp", "rec"), None),
    )
    return jax.shard_map(
        on_device, mesh=mesh, in_specs=in_specs, out_specs=out_specs, check_vma=False
    )
```

time: 741 us -> 462 us (0.62)
  matrix products: 173 us -> 61.4 us
  blocking collectives: 109 us -> 15.4 us
  waiting for transfers between devices: 409 us -> 341 us
    dot_general x5 -> x7, matrix products: 171 us -> 60.7 us  [the longest x1 46.3 us: on_device(): lax.dot_general(row_block, block, (((0,), (0,)), ((), ())), preferred_ele...]
    all_to_all x1 -> x0, blocking collectives: 109 us -> none  [on_device(): lax.all_to_all(records, 'rec', split_axis=1, concat_axis=0, tiled=True)]
    reduce_scatter x2 -> x0, waiting for transfers between devices: 60.5 us -> none  [on_device(): lax.psum_scatter(partial_value, 'smp', scatter_dimension=0, tiled=True)]
    all_gather x5 -> x2, waiting for transfers between devices: 232 us -> 185 us  [the longest x1 154 us: on_device(): block = lax.all_gather(records, 'rec', axis=0, tiled=True)]
    psum x2 -> x3, waiting for transfers between devices: 115 us -> 155 us  [the longest x1 80.9 us: on_device(): first = lax.psum(exact_dot(own, start_modes[0], 1), ('rec', 'smp'))]
    all_gather x0 -> x1, blocking collectives: none -> 15.4 us  [on_device(): second = lax.all_gather(second_own, 'rec', axis=0, tiled=True)]
  transfers between devices with their start and end apart: 9 -> 5, of which waited for: 9 -> 5; matrix products, arithmetic and copies ran while one was open for 7% -> 8% of each run, Pallas kernels for 0% -> 0%
where the time goes in v1:
time: 462 us
  waiting for transfers between devices  341 us (74%)
  matrix products  61.4 us (13%)
  other arithmetic  26.6 us (6%)
  blocking collectives  15.4 us (3%)
  between operations  13.9 us (3%)
    all_gather x1, waiting for transfers between devices, on_device(): block = lax.all_gather(records, 'rec', axis=0, tiled=True)  154 us
    psum x1, waiting for transfers between devices, on_device(): first = lax.psum(exact_dot(own, start_modes[0], 1), ('rec', 'smp'))  80.9 us
    dot_general x1, matrix products, on_device(): lax.dot_general(row_block, block, (((0,), (0,)), ((), ())), preferred_ele...  46.3 us
    psum x1, waiting for transfers between devices, on_device(): lax.psum(lax.dot_general(records, block, (((1,), (1,)), ((), ())), prefer...  39 us
    psum x1, waiting for transfers between devices, on_device(): lax.psum(jnp.dot(second_own.T, amplitude, precision=HIGHEST), 'rec') / total  34.9 us
    all_gather x1, waiting for transfers between devices, on_device(): row_block = lax.all_gather(own, 'smp', axis=1, tiled=True)  31.6 us
    all_gather x1, blocking collectives, on_device(): second = lax.all_gather(second_own, 'rec', axis=0, tiled=True)  15.4 us
    another operation x3, other arithmetic, on_device(): factor = jnp.linalg.cholesky(inner)  12.4 us
  transfers between devices with their start and end apart: 5, of which 5 were waited for; matrix products, arithmetic and copies ran while one was open for 8% of the time, Pallas kernels for 0%

profile of v1, /device:TPU:0, one launch (start us, length us, event | category | flops | bytes accessed | tf_op | source)
XLA Modules:
  0.0 461.6 jit_solution(16105982137509819281)
XLA Ops:
  7.2 0.0 copy-start.3
  7.2 0.0 all-gather.3.cloned.1.call-start
  7.2 0.7 all-gather.3.cloned.1.call-update
  7.9 0.0 all-reduce.6.cloned.1.call-start
  8.0 0.2 copy-done.3
  8.2 0.1 reduce-precision_convert_fusion.3
  8.3 153.6 %all-gather.3.cloned.1.call-done = bf16[1024,4096]{1,0:T(8,128)(2,1)} async-done(((bf16[256,4096]{1,0:T(8,128)(2,1)}), bf16[1024,4096]{1,0:T(8,128)(2,1)}) %all-gather.3.cloned.1.call-update) | async-done | bytes 8388624 | tf_op jit(solution)/shard_map/all_gather | solution.py:37
  161.9 1.8 constant_dynamic-slice_fusion
  163.7 0.0 copy-start
  163.7 1.2 fusion.4
  165.0 0.1 copy-done
  165.0 0.9 slice_add_fusion.2
  165.9 0.0 all-reduce.6.cloned.1.call-update
  165.9 0.0 all-reduce.4.cloned.1.call-start
  166.0 7.4 %fusion.34 = f32[256,1024]{1,0:T(8,128)} fusion(bf16[256,4096]{1,0:T(8,128)(2,1)} %param.2, bf16[1024,4096]{1,0:T(8,128)(2,1)} %all-gather.3.cloned.1.call-done), kind=kOutput, calls=%fused_computation.56 | convolution fusion | flops 2147483648 | bytes 11534336 | tf_op jit(solution)/shard_map/dot_general | solution.py:42
  173.4 0.0 all-reduce.4.cloned.1.call-update
  173.4 0.0 all-reduce.8.cloned.1.call-start
  173.4 80.9 %all-reduce.6.cloned.1.call-done = f32[1024,128]{1,0:T(8,128)} async-done(((f32[1024,128]{1,0:T(8,128)}), f32[1024,128]{1,0:T(8,128)}) %all-reduce.6.cloned.1.call-update) | async-done | bytes 524304 | tf_op jit(solution)/shard_map/psum | solution.py:47
  254.4 39.0 %all-reduce.4.cloned.1.call-done = f32[256,1024]{1,0:T(8,128)} async-done(((f32[256,1024]{1,0:T(8,128)}), f32[256,1024]{1,0:T(8,128)}) %all-reduce.4.cloned.1.call-update) | async-done | bytes 1048592 | tf_op jit(solution)/shard_map/psum | solution.py:41
  293.4 0.0 copy-start.2
  293.4 2.4 fusion.2
  295.8 15.4 %all_gather.11 = f32[1024,128]{1,0:T(8,128)S(1)} all-gather(f32[256,128]{1,0:T(8,128)S(1)} %fusion.2), channel_id=1, replica_groups=mesh['grp'=2,'rec'=4,'smp'=4] {'rec'}, dimensions={0}, use_global_device_ids=true | all-gather | bytes 655360 | tf_op jit(solution)/shard_map/all_gather | solution.py:49
  311.2 0.0 copy-done.2
  311.2 1.0 fusion
  312.2 1.0 fusion.35
  313.2 0.0 all-reduce.8.cloned.1.call-update
  313.2 0.2 all-gather.5.cloned.1.call-start
  313.5 0.4 all-gather.5.cloned.1.call-update
  313.8 0.0 copy-start.1
  313.8 34.9 %all-reduce.8.cloned.1.call-done = f32[128,128]{0,1:T(8,128)} async-done(((f32[128,128]{0,1:T(8,128)}), f32[128,128]{0,1:T(8,128)}) %all-reduce.8.cloned.1.call-update) | async-done | bytes 65552 | tf_op jit(solution)/shard_map/psum | solution.py:51
  348.8 0.8 broadcast_multiply_fusion
  349.6 0.1 copy.6
  349.7 0.9 fusion.28
  350.6 11.7 %cholesky.16 = f32[128,128]{1,0:T(8,128)S(1)} custom-call(f32[128,128]{1,0:T(8,128)S(1)} %fusion.28), custom_call_target="Cholesky" | custom-call | tf_op jit(solution)/shard_map/jit(cholesky)/cholesky | solution.py:61
  362.3 0.6 compare_reduce_fusion
  363.0 0.7 fusion.26
  363.6 9.8 %custom-call.6 = f32[1,128,128]{1,2,0:T(8,128)S(1)} custom-call(f32[1,128,128]{2,1,0:T(8,128)S(1)} %fusion.26), custom_call_target="InvertDiagBlocksLowerTriangular" | custom-call | tf_op jit(solution)/shard_map/triangular_solve | solution.py:62
  373.4 0.7 fusion.16
  374.2 0.8 copy.7
  374.9 0.1 reduce-precision_convert_fusion.1
  375.1 0.0 copy-done.1
  375.1 1.3 fusion.10
  376.4 0.9 fusion.23
  377.3 31.6 %all-gather.5.cloned.1.call-done = bf16[1024,4096]{1,0:T(8,128)(2,1)} async-done(((bf16[1024,1024]{1,0:T(8,128)(2,1)}), bf16[1024,4096]{1,0:T(8,128)(2,1)}) %all-gather.5.cloned.1.call-update) | async-done | bytes 8388624 | tf_op jit(solution)/shard_map/all_gather | solution.py:39
  408.9 46.3 %convolution_multiply_fusion = f32[4096,4096]{1,0:T(8,128)} fusion(bf16[1024,4096]{1,0:T(8,128)(2,1)} %all-gather.5.cloned.1.call-done, bf16[1024,4096]{1,0:T(8,128)(2,1)} %all-gather.3.cloned.1.call-done), kind=kOutput, calls=%fused_computation | convolution fusion | flops 34376515584 | bytes 83886080 | tf_op jit(solution)/shard_map/dot_general | solution.py:54
  (2 shorter events, 0.0 us)
Async XLA Ops:
  7.2 1.0 copy-start.3
  7.2 154.8 %all-gather.3.cloned.1.call-start = ((), (), s32[]{:S(2)}) async-start(), calls=%async_computation | async-start | bytes 10485760 | tf_op jit(solution)/shard_map/all_gather | solution.py:37
  7.9 246.5 %all-reduce.6.cloned.1.call-start = ((), (), s32[]{:S(2)}) async-start(), calls=%async_computation.3 | async-start | bytes 1048576 | tf_op jit(solution)/shard_map/psum | solution.py:47
  163.7 1.3 copy-start
  165.9 127.4 %all-reduce.4.cloned.1.call-start = ((), (), s32[]{:S(2)}) async-start(), calls=%async_computation.2 | async-start | bytes 2097152 | tf_op jit(solution)/shard_map/psum | solution.py:41
  173.4 175.4 %all-reduce.8.cloned.1.call-start = ((), (), s32[]{:S(2)}) async-start(), calls=%async_computation.4 | async-start | bytes 131072 | tf_op jit(solution)/shard_map/psum | solution.py:51
  293.4 17.8 %copy-start.2 = (f32[256,1024]{1,0:T(8,128)S(1)}, f32[256,1024]{1,0:T(8,128)}, u32[]{:S(2)}) copy-start(f32[256,1024]{1,0:T(8,128)} %all-reduce.4.cloned.1.call-done) | copy-start | bytes 3145732
  313.2 95.6 %all-gather.5.cloned.1.call-start = ((), (), s32[]{:S(2)}) async-start(), calls=%async_computation.1 | async-start | bytes 10485760 | tf_op jit(solution)/shard_map/all_gather | solution.py:39
  313.8 61.3 %copy-start.1 = (bf16[1024,1024]{1,0:T(8,128)(2,1)S(1)}, bf16[1024,1024]{1,0:T(8,128)(2,1)}, u32[]{:S(2)}) copy-start(bf16[1024,1024]{1,0:T(8,128)(2,1)} %copy-done) | copy-start | bytes 6291460
Sparse Core Ops, SparseCore 0:
  9.6 152.3 all-gather.2
  166.0 88.2 all-reduce.5
  256.8 36.5 all-reduce.3
  313.3 35.3 all-reduce.7
  350.7 58.0 all-gather.4

commit v2 on v1

--- a/solution.py
+++ b/solution.py
@@ -1,11 +1,252 @@
+import functools
 import math
 
 import jax
 import jax.numpy as jnp
 from jax import lax
+from jax.experimental import pallas as pl
+from jax.experimental.pallas import tpu as pltpu
 from jax.sharding import PartitionSpec as P
 
 HIGHEST = lax.Precision.HIGHEST
+
+
+def remote(src, dst, send_sem, recv_sem, device):
+    return pltpu.make_async_remote_copy(
+        src_ref=src,
+        dst_ref=dst,
+        send_sem=send_sem,
+        recv_sem=recv_sem,
+        device_id=device,
+        device_id_type=pl.DeviceIdType.MESH,
+    )
+
+
+def greet(devices):
+    barrier = pltpu.get_barrier_semaphore()
+    for device in devices:
+        pl.semaphore_signal(barrier, inc=1, device_id=device, device_id_type=pl.DeviceIdType.MESH)
+    pl.semaphore_wait(barrier, len(devices))
+
+
+def gather_kernel(n, m, rec_ref, block_ref, row_ref, up_sem, down_sem, in_sem, out_x, in_x, local):
+    g, r, s = lax.axis_index("grp"), lax.axis_index("rec"), lax.axis_index("smp")
+    rows, width = rec_ref.shape
+    sub = width // n
+    up, down = lax.rem(r + 1, n), lax.rem(r + n - 1, n)
+    across = [lax.rem(s + k, m) for k in range(1, m)]
+    greet([(g, up, s), (g, down, s)] + [(g, r, d) for d in across])
+
+    def spot(ref, b, q):
+        return ref.at[pl.ds(pl.multiple_of(b * rows, rows), rows), pl.ds(pl.multiple_of(q * sub, sub), sub)]
+
+    def chunk(b, q, own):
+        return rec_ref.at[:, pl.ds(q * sub, sub)] if own else spot(block_ref, b, q)
+
+    def send_up(b, q, own):
+        return remote(chunk(b, q, own), spot(block_ref, b, q), up_sem.at[b, q], in_sem.at[b, q], (g, up, s))
+
+    def send_down(b, q, own):
+        return remote(chunk(b, q, own), spot(block_ref, b, q), down_sem.at[b, q], in_sem.at[b, q], (g, down, s))
+
+    def mine(b, own):
+        if own:
+            return rec_ref.at[:, pl.ds(pl.multiple_of(r * sub, sub), sub)]
+        return spot(block_ref, b, r)
+
+    def send_across(b, k, own):
+        return remote(mine(b, own), spot(row_ref, b, s), out_x.at[k, b], in_x.at[k, b], (g, r, across[k]))
+
+    def keep(b, own):
+        return pltpu.make_async_copy(mine(b, own), spot(row_ref, b, s), local.at[b])
+
+    def spread(b, own):
+        for k in range(m - 1):
+            send_across(b, k, own).start()
+        keep(b, own).start()
+
+    whole = pltpu.make_async_copy(
+        rec_ref, block_ref.at[pl.ds(pl.multiple_of(r * rows, rows), rows)], local.at[n]
+    )
+    for i in range(n):
+        @pl.when(r < n - 1)
+        def _():
+            send_up(r, n - 1 - i, True).start()
+
+        @pl.when(r > 0)
+        def _():
+            send_down(r, i, True).start()
+
+    spread(r, True)
+    whole.start()
+    for t in range(1, n):
+        for i in range(n):
+            @pl.when(r + t < n)
+            def _():
+                b, q = r + t, i
+                send_down(b, q, False).wait_recv()
+
+                @pl.when(r > 0)
+                def _():
+                    send_down(b, q, False).start()
+
+                @pl.when(r == q)
+                def _():
+                    spread(b, False)
+
+            @pl.when(r - t >= 0)
+            def _():
+                b, q = r - t, n - 1 - i
+                send_up(b, q, False).wait_recv()
+
+                @pl.when(r < n - 1)
+                def _():
+                    send_up(b, q, False).start()
+
+                @pl.when(r == q)
+                def _():
+                    spread(b, False)
+
+    whole.wait()
+    for i in range(n):
+        @pl.when(r < n - 1)
+        def _():
+            send_up(r, i, True).wait_send()
+
+        @pl.when(r > 0)
+        def _():
+            send_down(r, i, True).wait_send()
+
+        for t in range(1, n):
+            @pl.when((r + t < n) & (r > 0))
+            def _():
+                send_down(r + t, i, False).wait_send()
+
+            @pl.when((r - t >= 0) & (r < n - 1))
+            def _():
+                send_up(r - t, i, False).wait_send()
+
+    for b in range(n):
+        pltpu.make_async_copy(spot(block_ref, b, r), spot(row_ref, b, s), local.at[b]).wait()
+        for k in range(m - 1):
+            copy = remote(
+                spot(block_ref, b, r), spot(row_ref, b, lax.rem(s + m - 1 - k, m)),
+                out_x.at[k, b], in_x.at[k, b], (g, r, across[k]),
+            )
+            copy.wait_send()
+            copy.wait_recv()
+
+
+def gather(records, n, m):
+    rows, width = records.shape
+    full = jax.ShapeDtypeStruct((rows * n, width), records.dtype)
+    wide = jax.ShapeDtypeStruct((rows * n, width // n * m), records.dtype)
+    dma = pltpu.SemaphoreType.DMA
+    return pl.pallas_call(
+        functools.partial(gather_kernel, n, m),
+        out_shape=(full, wide),
+        in_specs=[pl.BlockSpec(memory_space=pl.ANY)],
+        out_specs=(pl.BlockSpec(memory_space=pl.ANY), pl.BlockSpec(memory_space=pl.ANY)),
+        scratch_shapes=[
+            dma((n, n)), dma((n, n)), dma((n, n)), dma((m - 1, n)), dma((m - 1, n)), dma((n + 1,)),
+        ],
+        compiler_params=pltpu.CompilerParams(collective_id=0, has_side_effects=True),
+        name="gather_records",
+    )(records)
+
+
+def iterate_kernel(
+    total, x_ref, w_ref, t_ref, c_ref,
+    pair_in, cross_out, cross_in, z_out, z_in, w_out, w_in, t_out, t_in, c_out, c_in,
+    send_sem, recv_sem,
+):
+    g, r, s = lax.axis_index("grp"), lax.axis_index("rec"), lax.axis_index("smp")
+
+    def flip(a, bit):
+        return a + bit - 2 * bit * lax.rem(a // bit, 2)
+
+    r1, r2 = flip(r, 1), flip(r, 2)
+    s1, s2 = flip(s, 1), flip(s, 2)
+    r3 = flip(r2, 1)
+    greet([(g, r1, s), (g, r2, s), (g, r3, s), (g, r, s1), (g, r, s2)])
+    kept = w_ref.shape[2]
+
+    def swap(at, src, dst, device):
+        return remote(src, dst, send_sem.at[at], recv_sem.at[at], device)
+
+    first = swap(0, x_ref.at[s1], pair_in.at[0], (g, r, s1))
+    second = swap(1, x_ref.at[flip(s2, 1)], pair_in.at[1], (g, r, s1))
+    second.start()
+    first.start()
+    second.wait()
+    cross_out[...] = x_ref[s2] + pair_in[1]
+    cross = swap(2, cross_out, cross_in, (g, r, s2))
+    cross.start()
+    first.wait()
+    cross.wait()
+    strip = x_ref[s] + pair_in[0] + cross_in[...]
+    size = strip.shape[1] - kept
+    gram = strip[:, :size].T / total
+
+    def add_up(at, value, outs, ins, devices):
+        for i, device in enumerate(devices):
+            outs[i] = value
+            copy = swap(at + i, outs.at[i], ins.at[i], device)
+            copy.start()
+            copy.wait()
+            value = value + ins[i]
+        return value
+
+    rec_pair = [(g, r1, s), (g, r2, s)]
+    smp_pair = [(g, r, s1), (g, r, s2)]
+    start = add_up(3, strip[:, size:], z_out, z_in, rec_pair)
+    own = add_up(5, jnp.dot(gram, start, precision=HIGHEST), w_out, w_in, smp_pair)
+    w_ref[r] = own
+    copies = [
+        swap(7 + i, w_ref.at[r], w_ref.at[r], (g, d, s)) for i, d in enumerate((r1, r2, r3))
+    ]
+    for copy in copies:
+        copy.start()
+    for i, d in enumerate((r1, r2, r3)):
+        swap(7 + i, w_ref.at[d], w_ref.at[d], (g, d, s)).wait_recv()
+    amplitude = add_up(10, jnp.dot(gram, w_ref[s], precision=HIGHEST), t_out, t_in, smp_pair)
+    t_ref[...] = amplitude
+    inner = jnp.dot(own.T, amplitude, precision=HIGHEST) / total
+    c_ref[...] = add_up(12, inner, c_out, c_in, rec_pair)
+    for copy in copies:
+        copy.wait_send()
+
+
+def iterate(x, kept, n, m):
+    total, width = x.shape
+    rows = total // n
+    f32 = jnp.float32
+    vmem = pl.BlockSpec(memory_space=pltpu.VMEM)
+    pair = pltpu.VMEM((2, rows, kept), f32)
+    inner = pltpu.VMEM((2, kept, kept), f32)
+    w, t, c = pl.pallas_call(
+        functools.partial(iterate_kernel, total),
+        out_shape=(
+            jax.ShapeDtypeStruct((n, rows, kept), f32),
+            jax.ShapeDtypeStruct((rows, kept), f32),
+            jax.ShapeDtypeStruct((kept, kept), f32),
+        ),
+        in_specs=[vmem],
+        out_specs=(vmem, vmem, vmem),
+        scratch_shapes=[
+            pltpu.VMEM((2, rows, width), f32),
+            pltpu.VMEM((rows, width), f32),
+            pltpu.VMEM((rows, width), f32),
+            pair, pair, pair, pair, pair, pair, inner, inner,
+            pltpu.SemaphoreType.DMA((14,)),
+            pltpu.SemaphoreType.DMA((14,)),
+        ],
+        compiler_params=pltpu.CompilerParams(
+            collective_id=1, has_side_effects=True, vmem_limit_bytes=32 * 2**20
+        ),
+        name="iterate_modes",
+    )(x.reshape(m, rows, width))
+    return w.reshape(total, kept), t, c
 
 
 def pieces(block):
@@ -34,21 +275,30 @@
     full_width = width * panels
     at = lax.axis_index("rec")
 
-    block = lax.all_gather(records, "rec", axis=0, tiled=True)
+    n, m = lax.axis_size("rec"), panels
+    direct = n == 4 and m == 4 and sub_width % 128 == 0 and rec_dev % 128 == 0 and kept % 128 == 0
+    if direct:
+        block, row_block = gather(records, n, m)
+    else:
+        block = lax.all_gather(records, "rec", axis=0, tiled=True)
     own = lax.dynamic_slice_in_dim(block, at * sub_width, sub_width, axis=1)
-    row_block = lax.all_gather(own, "smp", axis=1, tiled=True)
-
-    gram = lax.psum(
-        lax.dot_general(
-            records, block, (((1,), (1,)), ((), ())), preferred_element_type=jnp.float32
-        ),
-        "smp",
-    ) / total
-    first = lax.psum(exact_dot(own, start_modes[0], 1), ("rec", "smp"))
-    second_own = jnp.dot(gram, first, precision=HIGHEST)
-    second = lax.all_gather(second_own, "rec", axis=0, tiled=True)
-    amplitude = jnp.dot(gram, second, precision=HIGHEST)
-    inner = lax.psum(jnp.dot(second_own.T, amplitude, precision=HIGHEST), "rec") / total
+    if not direct:
+        row_block = lax.all_gather(own, "smp", axis=1, tiled=True)
+
+    gram_part = lax.dot_general(
+        block, records, (((1,), (1,)), ((), ())), preferred_element_type=jnp.float32
+    )
+    first_part = exact_dot(own, start_modes[0], 1)
+    if direct:
+        stacked = jnp.concatenate([gram_part, first_part], axis=1)
+        second, amplitude, inner = iterate(stacked, kept, n, m)
+    else:
+        gram = lax.psum(gram_part, "smp").T / total
+        first = lax.psum(first_part, ("rec", "smp"))
+        second_own = jnp.dot(gram, first, precision=HIGHEST)
+        second = lax.all_gather(second_own, "rec", axis=0, tiled=True)
+        amplitude = jnp.dot(gram, second, precision=HIGHEST)
+        inner = lax.psum(jnp.dot(second_own.T, amplitude, precision=HIGHEST), "rec") / total
 
     tile = (
         lax.dot_general(

time: 462 us -> 286 us (0.62)
  waiting for transfers between devices: 341 us -> 0 us
  Pallas kernels: 0 us -> 199 us
  blocking collectives: 15.4 us -> 0 us
  between operations: 13.9 us -> 0.76 us
    pallas_call x0 -> x2, Pallas kernels: none -> 199 us  [the longest x1 141 us: gather(): pl.pallas_call(functools.partial(gather_kernel, n, m), out_shape=(full, w...]
    all_gather x2 -> x0, waiting for transfers between devices: 185 us -> none  [the longest x1 154 us: on_device(): block = lax.all_gather(records, 'rec', axis=0, tiled=True)]
    psum x3 -> x0, waiting for transfers between devices: 155 us -> none  [the longest x1 80.9 us: on_device(): first = lax.psum(exact_dot(own, start_modes[0], 1), ('rec', 'smp'))]
    all_gather x1 -> x0, blocking collectives: 15.4 us -> none  [on_device(): second = lax.all_gather(second_own, 'rec', axis=0, tiled=True)]
    dot_general x4 -> x1, matrix products: 11.8 us -> 5.99 us  [on_device(): lax.dot_general(block, records, (((1,), (1,)), ((), ())), preferred_eleme...]
  transfers between devices with their start and end apart: 5 -> 0, of which waited for: 5 -> 0; matrix products, arithmetic and copies ran while one was open for 8% -> 0% of each run, Pallas kernels for 0% -> 0%
where the time goes in v2:
time: 286 us; the launch traced here: 285 us
  Pallas kernels  199 us (70%)
  matrix products  58.6 us (20%)
  other arithmetic  24.2 us (8%)
    pallas_call x1, Pallas kernels, gather(): pl.pallas_call(functools.partial(gather_kernel, n, m), out_shape=(full, w...  141 us
    pallas_call x1, Pallas kernels, iterate(): pl.pallas_call(functools.partial(iterate_kernel, total), out_shape=(jax.S...  57.5 us
    dot_general x1, matrix products, on_device(): lax.dot_general(row_block, block, (((0,), (0,)), ((), ())), preferred_ele...  46.3 us
    another operation x3, other arithmetic, on_device(): factor = jnp.linalg.cholesky(inner)  12.4 us
    another operation x2, other arithmetic, on_device(): lax.linalg.triangular_solve(factor, jnp.concatenate([second, amplitude],...  10.5 us
    dot_general x1, matrix products, on_device(): lax.dot_general(block, records, (((1,), (1,)), ((), ())), preferred_eleme...  5.99 us

profile of v2, /device:TPU:0, one launch (start us, length us, event | category | flops | bytes accessed | tf_op | source)
XLA Modules:
  0.0 285.3 jit_solution(561755387194949794)
XLA Ops:
  0.6 141.5 %gather_records.1 = (bf16[1024,4096]{1,0:T(8,128)(2,1)}, bf16[1024,4096]{1,0:T(8,128)(2,1)}) custom-call(bf16[256,4096]{1,0:T(8,128)(2,1)} %rec_ref.1), custom_call_target="tpu_custom_call" | custom-call | tf_op jit(solution)/shard_map/gather_records/pallas_call | solution.py:145
  142.1 0.0 copy-start.1
  142.1 46.3 %convolution_multiply_fusion = f32[4096,4096]{1,0:T(8,128)} fusion(bf16[1024,4096]{1,0:T(8,128)(2,1)} %get-tuple-element.8, bf16[1024,4096]{1,0:T(8,128)(2,1)} %get-tuple-element.9), kind=kOutput, calls=%fused_computation | convolution fusion | flops 34376515584 | bytes 83886080 | tf_op jit(solution)/shard_map/dot_general | solution.py:304
  188.4 0.0 copy-done.1
  188.4 0.1 reduce-precision_convert_fusion.3
  188.6 2.6 fusion.2
  191.2 0.0 copy-start
  191.2 0.1 slice_add_fusion.2
  191.3 1.5 copy-done
  192.8 6.0 %fusion.30 = f32[1024,256]{0,1:T(8,128)S(1)} fusion(bf16[1024,4096]{1,0:T(8,128)(2,1)} %get-tuple-element.9, bf16[256,4096]{1,0:T(8,128)(2,1)S(1)} %copy-done), kind=kOutput, calls=%fused_computation.51 | convolution fusion | flops 2147483648 | bytes 11534336 | tf_op jit(solution)/shard_map/dot_general | solution.py:288
  198.8 0.1 pad_maximum_fusion
  198.9 0.5 copy.5
  199.4 57.5 %iterate_modes.1 = (f32[4,256,128]{2,1,0:T(8,128)S(1)}, f32[256,128]{1,0:T(8,128)S(1)}, f32[128,128]{1,0:T(8,128)S(1)}) custom-call(f32[4,256,384]{2,1,0:T(8,128)S(1)} %bitcast.25), custom_call_target="tpu_custom_call" | custom-call | tf_op jit(solution)/shard_map/iterate_modes/pallas_call | solution.py:227
  256.9 0.1 copy.6
  257.0 11.7 %cholesky.16 = f32[128,128]{1,0:T(8,128)S(1)} custom-call(f32[128,128]{1,0:T(8,128)S(1)} %fusion.24), custom_call_target="Cholesky" | custom-call | tf_op jit(solution)/shard_map/jit(cholesky)/cholesky | solution.py:311
  268.7 0.6 compare_reduce_fusion
  269.4 0.7 fusion.22
  270.0 9.8 %custom-call.6 = f32[1,128,128]{1,2,0:T(8,128)S(1)} custom-call(f32[1,128,128]{2,1,0:T(8,128)S(1)} %fusion.22), custom_call_target="InvertDiagBlocksLowerTriangular" | custom-call | tf_op jit(solution)/shard_map/triangular_solve | solution.py:312
  279.9 0.7 fusion.14
  280.6 0.1 reduce-precision_convert_fusion.1
  280.7 2.9 %fusion = f32[1024,384]{1,0:T(8,128)S(1)} fusion(bf16[1024,4096]{1,0:T(8,128)(2,1)} %get-tuple-element.9, s32[]{:T(128)S(6)} %select_n.7, bf16[1024,128]{0,1:T(8,128)(2,1)S(1)} %get-tuple-element.17, bf16[1024,128]{0,1:T(8,128)(2,1)S(1)} %get-tuple-element.18, bf16[1024,128]{0,1:T(8,128)(2,1)S(1)} %get-tuple-element.16), kind=kOutput, calls=%fused_computation.1 | convolution fusion | flops 807665664 | bytes 4456452 | tf_op jit(solution)/shard_map/dot_general | solution.py:264
  283.6 0.9 fusion.21
  284.5 0.8 copy.7
  (3 shorter events, 0.1 us)
Async XLA Ops:
  142.1 46.3 %copy-start.1 = (f32[1,1024,128]{2,1,0:T(8,128)S(1)}, f32[1,1024,128]{2,1,0:T(8,128)}, u32[]{:S(2)}) copy-start(f32[1,1024,128]{2,1,0:T(8,128)} %param.3) | copy-start | bytes 1572868
  191.2 1.6 copy-start

commit v3 on v2

--- a/solution.py
+++ b/solution.py
@@ -155,98 +155,85 @@
     )(records)
 
 
-def iterate_kernel(
-    total, x_ref, w_ref, t_ref, c_ref,
-    pair_in, cross_out, cross_in, z_out, z_in, w_out, w_in, t_out, t_in, c_out, c_in,
-    send_sem, recv_sem,
-):
-    g, r, s = lax.axis_index("grp"), lax.axis_index("rec"), lax.axis_index("smp")
-
-    def flip(a, bit):
-        return a + bit - 2 * bit * lax.rem(a // bit, 2)
-
-    r1, r2 = flip(r, 1), flip(r, 2)
-    s1, s2 = flip(s, 1), flip(s, 2)
-    r3 = flip(r2, 1)
-    greet([(g, r1, s), (g, r2, s), (g, r3, s), (g, r, s1), (g, r, s2)])
-    kept = w_ref.shape[2]
-
-    def swap(at, src, dst, device):
-        return remote(src, dst, send_sem.at[at], recv_sem.at[at], device)
-
-    first = swap(0, x_ref.at[s1], pair_in.at[0], (g, r, s1))
-    second = swap(1, x_ref.at[flip(s2, 1)], pair_in.at[1], (g, r, s1))
-    second.start()
-    first.start()
-    second.wait()
-    cross_out[...] = x_ref[s2] + pair_in[1]
-    cross = swap(2, cross_out, cross_in, (g, r, s2))
-    cross.start()
-    first.wait()
-    cross.wait()
-    strip = x_ref[s] + pair_in[0] + cross_in[...]
-    size = strip.shape[1] - kept
-    gram = strip[:, :size].T / total
-
-    def add_up(at, value, outs, ins, devices):
-        for i, device in enumerate(devices):
-            outs[i] = value
-            copy = swap(at + i, outs.at[i], ins.at[i], device)
-            copy.start()
-            copy.wait()
-            value = value + ins[i]
-        return value
-
-    rec_pair = [(g, r1, s), (g, r2, s)]
-    smp_pair = [(g, r, s1), (g, r, s2)]
-    start = add_up(3, strip[:, size:], z_out, z_in, rec_pair)
-    own = add_up(5, jnp.dot(gram, start, precision=HIGHEST), w_out, w_in, smp_pair)
-    w_ref[r] = own
-    copies = [
-        swap(7 + i, w_ref.at[r], w_ref.at[r], (g, d, s)) for i, d in enumerate((r1, r2, r3))
-    ]
-    for copy in copies:
-        copy.start()
-    for i, d in enumerate((r1, r2, r3)):
-        swap(7 + i, w_ref.at[d], w_ref.at[d], (g, d, s)).wait_recv()
-    amplitude = add_up(10, jnp.dot(gram, w_ref[s], precision=HIGHEST), t_out, t_in, smp_pair)
-    t_ref[...] = amplitude
-    inner = jnp.dot(own.T, amplitude, precision=HIGHEST) / total
-    c_ref[...] = add_up(12, inner, c_out, c_in, rec_pair)
-    for copy in copies:
-        copy.wait_send()
+def flip(a, bit):
+    return a + bit - 2 * bit * lax.rem(a // bit, 2)
+
+
+def swap(value, axis, bit):
+    return lax.ppermute(value, axis, [(i, i ^ bit) for i in range(lax.axis_size(axis))])
+
+
+def add_up(value, axis):
+    for bit in (1, 2):
+        value = value + swap(value, axis, bit)
+    return value
 
 
 def iterate(x, kept, n, m):
     total, width = x.shape
     rows = total // n
-    f32 = jnp.float32
-    vmem = pl.BlockSpec(memory_space=pltpu.VMEM)
-    pair = pltpu.VMEM((2, rows, kept), f32)
-    inner = pltpu.VMEM((2, kept, kept), f32)
-    w, t, c = pl.pallas_call(
-        functools.partial(iterate_kernel, total),
-        out_shape=(
-            jax.ShapeDtypeStruct((n, rows, kept), f32),
-            jax.ShapeDtypeStruct((rows, kept), f32),
-            jax.ShapeDtypeStruct((kept, kept), f32),
+    r, s = lax.axis_index("rec"), lax.axis_index("smp")
+    x = x.reshape(m, rows, width)
+
+    def strip_of(at):
+        return lax.dynamic_index_in_dim(x, at, 0, keepdims=False)
+
+    s1, s2 = flip(s, 1), flip(s, 2)
+    far = strip_of(s2) + swap(strip_of(flip(s2, 1)), "smp", 1)
+    near = strip_of(s) + swap(strip_of(s1), "smp", 1)
+    strip = near + swap(far, "smp", 2)
+    gram = strip[:, :rows].T / total
+    start = add_up(strip[:, rows:], "rec")
+    own = add_up(jnp.dot(gram, start, precision=HIGHEST), "smp")
+    others = [swap(own, "rec", bit) for bit in (1, 2, 3)]
+    second = jnp.zeros((n, rows, kept), jnp.float32)
+    for at, value in zip((r, flip(r, 1), flip(r, 2), flip(flip(r, 2), 1)), [own] + others):
+        second = lax.dynamic_update_index_in_dim(second, value, at, 0)
+    here = lax.dynamic_index_in_dim(second, s, 0, keepdims=False)
+    amplitude = add_up(jnp.dot(gram, here, precision=HIGHEST), "smp")
+    inner = add_up(jnp.dot(own.T, amplitude, precision=HIGHEST) / total, "rec")
+    return second.reshape(total, kept), amplitude, inner
+
+
+def panel_kernel(total, left_ref, right_ref, *rest):
+    out_ref, turned = rest[-2:]
+
+    @pl.when(pl.program_id(0) == 0)
+    def _():
+        turned[...] = left_ref[...].T
+
+    out_ref[...] = (
+        jnp.dot(turned[...], right_ref[...], preferred_element_type=jnp.float32) * (1.0 / total)
+    )
+
+
+def covariance_panel(row_block, block, tile, at, height):
+    total, width = block.shape
+    across = 512
+    in_specs = [
+        pl.BlockSpec((total, height), lambda j: (0, at)),
+        pl.BlockSpec((total, across), lambda j: (0, j)),
+    ]
+    args = [row_block, block]
+    if tile is not None:
+        in_specs.append(pl.BlockSpec(memory_space=pl.ANY))
+        args.append(tile)
+    return pl.pallas_call(
+        functools.partial(panel_kernel, total),
+        out_shape=jax.ShapeDtypeStruct((row_block.shape[1], width), jnp.float32),
+        grid=(width // across,),
+        in_specs=in_specs,
+        out_specs=pl.BlockSpec((height, across), lambda j: (at, j)),
+        scratch_shapes=[pltpu.VMEM((height, total), jnp.bfloat16)],
+        input_output_aliases={} if tile is None else {2: 0},
+        compiler_params=pltpu.CompilerParams(vmem_limit_bytes=32 * 2**20),
+        cost_estimate=pl.CostEstimate(
+            flops=2 * total * height * width,
+            bytes_accessed=4 * height * width + 2 * total * (height + width),
+            transcendentals=0,
         ),
-        in_specs=[vmem],
-        out_specs=(vmem, vmem, vmem),
-        scratch_shapes=[
-            pltpu.VMEM((2, rows, width), f32),
-            pltpu.VMEM((rows, width), f32),
-            pltpu.VMEM((rows, width), f32),
-            pair, pair, pair, pair, pair, pair, inner, inner,
-            pltpu.SemaphoreType.DMA((14,)),
-            pltpu.SemaphoreType.DMA((14,)),
-        ],
-        compiler_params=pltpu.CompilerParams(
-            collective_id=1, has_side_effects=True, vmem_limit_bytes=32 * 2**20
-        ),
-        name="iterate_modes",
-    )(x.reshape(m, rows, width))
-    return w.reshape(total, kept), t, c
+        name="covariance_panel",
+    )(*args)
 
 
 def pieces(block):
@@ -276,7 +263,8 @@
     at = lax.axis_index("rec")
 
     n, m = lax.axis_size("rec"), panels
-    direct = n == 4 and m == 4 and sub_width % 128 == 0 and rec_dev % 128 == 0 and kept % 128 == 0
+    direct = n == 4 and m == 4 and sub_width % 256 == 0 and width % 512 == 0 and rec_dev % 128 == 0
+    direct = direct and kept % 128 == 0
     if direct:
         block, row_block = gather(records, n, m)
     else:
@@ -300,12 +288,18 @@
         amplitude = jnp.dot(gram, second, precision=HIGHEST)
         inner = lax.psum(jnp.dot(second_own.T, amplitude, precision=HIGHEST), "rec") / total
 
-    tile = (
-        lax.dot_general(
-            row_block, block, (((0,), (0,)), ((), ())), preferred_element_type=jnp.float32
+    if direct:
+        tile = None
+        height = sub_width // 2
+        for piece in range(2 * panels):
+            tile = covariance_panel(row_block, block, tile, piece, height)
+    else:
+        tile = (
+            lax.dot_general(
+                row_block, block, (((0,), (0,)), ((), ())), preferred_element_type=jnp.float32
+            )
+            / total
         )
-        / total
-    )
     covariance = tile.reshape(panels, sub_width, width)
 
     factor = jnp.linalg.cholesky(inner)

time: 286 us -> 311 us (1.087)
  matrix products: 58.6 us -> 13.2 us
  waiting for transfers between devices: 0 us -> 25.5 us
  local copies, waits for them, and re-layouts: 2.81 us -> 23.4 us
  starting transfers between devices: 0 us -> 13 us
  Pallas kernels: 199 us -> 208 us
    dot_general x1 -> x3, matrix products: 46.3 us -> 1.14 us  [the longest x1 0.39 us: iterate(): inner = add_up(jnp.dot(own.T, amplitude, precision=HIGHEST) / total, 'rec')]
    ppermute x0 -> x14, waiting for transfers between devices: none -> 25.5 us  [swap(): lax.ppermute(value, axis, [(i, i ^ bit) for i in range(lax.axis_size(axis...]
    unnamed x5 -> x21, local copies, waits for them, and re-layouts: 2.25 us -> 21.1 us
    ppermute x0 -> x14, starting transfers between devices: none -> 13 us  [swap(): lax.ppermute(value, axis, [(i, i ^ bit) for i in range(lax.axis_size(axis...]
    pallas_call x1 -> x8, Pallas kernels: 57.5 us -> 66.4 us  [covariance_panel(): pl.pallas_call(functools.partial(panel_kernel, total), out_shape=jax.Shap...]
  transfers between devices with their start and end apart: 0 -> 14, of which waited for: 0 -> 4; matrix products, arithmetic and copies ran while one was open for 0% -> 0% of each run, Pallas kernels for 0% -> 21%
where the time goes in v3:
time: 311 us; the launch traced here: 310 us
  Pallas kernels  208 us (67%)
  other arithmetic  26.3 us (8%)
  waiting for transfers between devices  25.5 us (8%)
  local copies, waits for them, and re-layouts  23.4 us (8%)
  matrix products  13.2 us (4%)
  starting transfers between devices  13 us (4%)
    pallas_call x1, Pallas kernels, gather(): pl.pallas_call(functools.partial(gather_kernel, n, m), out_shape=(full, w...  141 us
    pallas_call x8, Pallas kernels, covariance_panel(): pl.pallas_call(functools.partial(panel_kernel, total), out_shape=jax.Shap...  66.4 us
    ppermute x14, waiting for transfers between devices, swap(): lax.ppermute(value, axis, [(i, i ^ bit) for i in range(lax.axis_size(axis...  25.5 us
    unnamed x21, local copies, waits for them, and re-layouts  21.1 us
    ppermute x14, starting transfers between devices, swap(): lax.ppermute(value, axis, [(i, i ^ bit) for i in range(lax.axis_size(axis...  13 us
    another operation x3, other arithmetic, on_device(): factor = jnp.linalg.cholesky(inner)  12.4 us
    another operation x2, other arithmetic, on_device(): lax.linalg.triangular_solve(factor, jnp.concatenate([second, amplitude],...  10.5 us
  transfers between devices with their start and end apart: 14, of which 4 were waited for; matrix products, arithmetic and copies ran while one was open for 0% of the time, Pallas kernels for 21%

profile of v3, /device:TPU:0, one launch (start us, length us, event | category | flops | bytes accessed | tf_op | source)
XLA Modules:
  0.0 310.3 jit_solution(9668858341469167803)
XLA Ops:
  0.7 141.5 %gather_records.1 = (bf16[1024,4096]{1,0:T(8,128)(2,1)}, bf16[1024,4096]{1,0:T(8,128)(2,1)}) custom-call(bf16[256,4096]{1,0:T(8,128)(2,1)} %rec_ref.1), custom_call_target="tpu_custom_call" | custom-call | tf_op jit(solution)/shard_map/gather_records/pallas_call | solution.py:145
  142.2 2.0 reduce-precision_convert_fusion.3
  144.1 5.7 %fusion.41 = f32[1024,256]{0,1:T(8,128)S(1)} fusion(bf16[1024,4096]{1,0:T(8,128)(2,1)} %get-tuple-element.6.right_ref, bf16[256,4096]{1,0:T(8,128)(2,1)S(1)} %copy-done.8), kind=kOutput, calls=%fused_computation.76 | convolution fusion | flops 2147483648 | bytes 11534336 | tf_op jit(solution)/shard_map/dot_general | solution.py:276
  149.9 2.7 fusion.2
  152.6 0.1 slice_add_fusion.2
  152.7 0.2 pad_maximum_fusion
  152.9 0.7 reshape.28
  153.6 1.4 constant_dynamic-slice_fusion.3
  155.2 0.6 collective-permute-start
  155.7 1.1 collective-permute-done.1
  156.9 1.0 collective-permute-start.2
  157.9 10.2 %collective-permute-done.2 = f32[256,384]{0,1:T(8,128)S(1)} collective-permute-done((f32[256,384]{0,1:T(8,128)S(1)}, f32[256,384]{0,1:T(8,128)S(1)}, u32[]{:S(2)}, u32[]{:S(2)}) %collective-permute-start.2) | collective-permute-done | bytes 393248 | tf_op jit(solution)/shard_map/ppermute | solution.py:163
  168.3 5.0 %collective-permute-done.3 = f32[256,128]{0,1:T(8,128)S(1)} collective-permute-done((f32[256,128]{0,1:T(8,128)S(1)}, f32[256,128]{0,1:T(8,128)S(1)}, u32[]{:S(2)}, u32[]{:S(2)}) %collective-permute-start.3) | collective-permute-done | bytes 131104 | tf_op jit(solution)/shard_map/ppermute | solution.py:163
  173.3 1.1 collective-permute-start.4
  174.4 3.4 %copy-done = bf16[1024,4096]{1,0:T(8,128)(2,1)S(1)} copy-done((bf16[1024,4096]{1,0:T(8,128)(2,1)S(1)}, bf16[1024,4096]{1,0:T(8,128)(2,1)}, u32[]{:S(2)}) %copy-start) | copy-done | bytes 8388632
  177.7 3.4 %copy-done.3 = bf16[1024,4096]{1,0:T(8,128)(2,1)S(1)} copy-done((bf16[1024,4096]{1,0:T(8,128)(2,1)S(1)}, bf16[1024,4096]{1,0:T(8,128)(2,1)}, u32[]{:S(2)}) %copy-start.3) | copy-done | bytes 8388632
  181.1 8.3 %covariance_panel.8.rest_0_ = f32[4096,4096]{1,0:T(8,128)} custom-call(bf16[1024,4096]{1,0:T(8,128)(2,1)S(1)} %copy-done.3, bf16[1024,4096]{1,0:T(8,128)(2,1)S(1)} %copy-done), custom_call_target="tpu_custom_call" | custom-call | flops 4294967296 | bytes 17825792 | tf_op jit(solution)/shard_map/covariance_panel/pallas_call | solution.py:221
  189.4 0.4 fusion.24
  189.9 8.3 %covariance_panel.9.rest_0_ = f32[4096,4096]{1,0:T(8,128)} custom-call(bf16[1024,4096]{1,0:T(8,128)(2,1)S(1)} %copy-done.3, bf16[1024,4096]{1,0:T(8,128)(2,1)S(1)} %copy-done, f32[4096,4096]{1,0:T(8,128)} %covariance_panel.8.rest_0_), custom_call_target="tpu_custom_call", output_to_operand_aliasing={{}: (2, {})} | custom-call | flops 4294967296 | bytes 17825792 | tf_op jit(solution)/shard_map/covariance_panel/pallas_call | solution.py:221
  198.2 1.0 collective-permute-start.6
  199.3 8.3 %covariance_panel.10.rest_0_ = f32[4096,4096]{1,0:T(8,128)} custom-call(bf16[1024,4096]{1,0:T(8,128)(2,1)S(1)} %copy-done.3, bf16[1024,4096]{1,0:T(8,128)(2,1)S(1)} %copy-done, f32[4096,4096]{1,0:T(8,128)} %covariance_panel.9.rest_0_), custom_call_target="tpu_custom_call", output_to_operand_aliasing={{}: (2, {})} | custom-call | flops 4294967296 | bytes 17825792 | tf_op jit(solution)/shard_map/covariance_panel/pallas_call | solution.py:221
  207.6 2.1 collective-permute-start.7
  209.7 3.4 %copy-done.1 = bf16[1024,4096]{1,0:T(8,128)(2,1)S(1)} copy-done((bf16[1024,4096]{1,0:T(8,128)(2,1)S(1)}, bf16[1024,4096]{1,0:T(8,128)(2,1)}, u32[]{:S(2)}) %copy-start.1) | copy-done | bytes 8388632
  213.1 3.4 %copy-done.4 = bf16[1024,4096]{1,0:T(8,128)(2,1)S(1)} copy-done((bf16[1024,4096]{1,0:T(8,128)(2,1)S(1)}, bf16[1024,4096]{1,0:T(8,128)(2,1)}, u32[]{:S(2)}) %copy-start.4) | copy-done | bytes 8388632
  216.5 8.3 %covariance_panel.11.rest_0_ = f32[4096,4096]{1,0:T(8,128)} custom-call(bf16[1024,4096]{1,0:T(8,128)(2,1)S(1)} %copy-done.4, bf16[1024,4096]{1,0:T(8,128)(2,1)S(1)} %copy-done.1, f32[4096,4096]{1,0:T(8,128)} %covariance_panel.10.rest_0_), custom_call_target="tpu_custom_call", output_to_operand_aliasing={{}: (2, {})} | custom-call | flops 4294967296 | bytes 17825792 | tf_op jit(solution)/shard_map/covariance_panel/pallas_call | solution.py:221
  224.8 2.4 collective-permute-start.9
  227.2 9.3 %collective-permute-done.8 = f32[256,128]{1,0:T(8,128)S(1)} collective-permute-done((f32[256,128]{1,0:T(8,128)S(1)}, f32[256,128]{1,0:T(8,128)S(1)}, u32[]{:S(2)}, u32[]{:S(2)}) %collective-permute-start.8) | collective-permute-done | bytes 131104 | tf_op jit(solution)/shard_map/ppermute | solution.py:163
  236.5 0.4 fusion.23
  236.9 3.4 %copy-done.2 = bf16[1024,4096]{1,0:T(8,128)(2,1)S(1)} copy-done((bf16[1024,4096]{1,0:T(8,128)(2,1)S(1)}, bf16[1024,4096]{1,0:T(8,128)(2,1)}, u32[]{:S(2)}) %copy-start.2) | copy-done | bytes 8388632
  240.3 3.4 %copy-done.5 = bf16[1024,4096]{1,0:T(8,128)(2,1)S(1)} copy-done((bf16[1024,4096]{1,0:T(8,128)(2,1)S(1)}, bf16[1024,4096]{1,0:T(8,128)(2,1)}, u32[]{:S(2)}) %copy-start.5) | copy-done | bytes 8388632
  243.7 8.3 %covariance_panel.12.rest_0_ = f32[4096,4096]{1,0:T(8,128)} custom-call(bf16[1024,4096]{1,0:T(8,128)(2,1)S(1)} %copy-done.5, bf16[1024,4096]{1,0:T(8,128)(2,1)S(1)} %copy-done.2, f32[4096,4096]{1,0:T(8,128)} %covariance_panel.11.rest_0_), custom_call_target="tpu_custom_call", output_to_operand_aliasing={{}: (2, {})} | custom-call | flops 4294967296 | bytes 17825792 | tf_op jit(solution)/shard_map/covariance_panel/pallas_call | solution.py:221
  252.0 1.1 collective-permute-start.11
  253.1 8.3 %covariance_panel.13.rest_0_ = f32[4096,4096]{1,0:T(8,128)} custom-call(bf16[1024,4096]{1,0:T(8,128)(2,1)S(1)} %copy-done.5, bf16[1024,4096]{1,0:T(8,128)(2,1)S(1)} %copy-done.2, f32[4096,4096]{1,0:T(8,128)} %covariance_panel.12.rest_0_), custom_call_target="tpu_custom_call", output_to_operand_aliasing={{}: (2, {})} | custom-call | flops 4294967296 | bytes 17825792 | tf_op jit(solution)/shard_map/covariance_panel/pallas_call | solution.py:221
  261.5 0.4 convolution_multiply_fusion
  261.9 3.3 %collective-permute-start.12 = (f32[128,128]{0,1:T(8,128)S(1)}, f32[128,128]{0,1:T(8,128)S(1)}, u32[]{:S(2)}, u32[]{:S(2)}) collective-permute-start(f32[128,128]{0,1:T(8,128)S(1)} %convolution_multiply_fusion), channel_id=1, source_target_pairs={{0,4},{4,0},{8,12},{12,8},{1,5},{5,1},{9,13},{13,9},{2,6},{6,2},{1... | collective-permute-start | bytes 196616 | tf_op jit(solution)/shard_map/ppermute | solution.py:163
  265.2 8.3 %covariance_panel.14.rest_0_ = f32[4096,4096]{1,0:T(8,128)} custom-call(bf16[1024,4096]{1,0:T(8,128)(2,1)S(1)} %copy-done.5, bf16[1024,4096]{1,0:T(8,128)(2,1)S(1)} %copy-done.2, f32[4096,4096]{1,0:T(8,128)} %covariance_panel.13.rest_0_), custom_call_target="tpu_custom_call", output_to_operand_aliasing={{}: (2, {})} | custom-call | flops 4294967296 | bytes 17825792 | tf_op jit(solution)/shard_map/covariance_panel/pallas_call | solution.py:221
  273.5 0.1 collective-permute-start.13
  273.6 8.3 %covariance_panel.15 = f32[4096,4096]{1,0:T(8,128)} custom-call(bf16[1024,4096]{1,0:T(8,128)(2,1)S(1)} %copy-done.5, bf16[1024,4096]{1,0:T(8,128)(2,1)S(1)} %copy-done.2, f32[4096,4096]{1,0:T(8,128)} %covariance_panel.14.rest_0_), custom_call_target="tpu_custom_call", output_to_operand_aliasing={{}: (2, {})} | custom-call | flops 4294967296 | bytes 17825792 | tf_op jit(solution)/shard_map/covariance_panel/pallas_call | solution.py:221
  281.9 0.1 copy.13
  282.0 11.7 %cholesky.16 = f32[128,128]{1,0:T(8,128)S(1)} custom-call(f32[128,128]{1,0:T(8,128)S(1)} %fusion.32), custom_call_target="Cholesky" | custom-call | tf_op jit(solution)/shard_map/jit(cholesky)/cholesky | solution.py:305
  293.8 0.6 compare_reduce_fusion
  294.4 0.7 fusion.30
  295.1 9.8 %custom-call.6 = f32[1,128,128]{1,2,0:T(8,128)S(1)} custom-call(f32[1,128,128]{2,1,0:T(8,128)S(1)} %fusion.30), custom_call_target="InvertDiagBlocksLowerTriangular" | custom-call | tf_op jit(solution)/shard_map/triangular_solve | solution.py:306
  304.9 0.7 fusion.14
  305.6 0.1 reduce-precision_convert_fusion.1
  305.8 2.9 fusion
  308.7 0.9 fusion.21
  309.6 0.8 copy.14
  (46 shorter events, 0.8 us)
Async XLA Ops:
  0.6 143.5 %copy-start.8 = (bf16[256,4096]{1,0:T(8,128)(2,1)S(1)}, bf16[256,4096]{1,0:T(8,128)(2,1)}, u32[]{:S(2)}) copy-start(bf16[256,4096]{1,0:T(8,128)(2,1)} %rec_ref.1) | copy-start | bytes 6291460
  155.0 1.8 collective-permute-start.1
  155.2 2.8 collective-permute-start
  156.9 11.2 %collective-permute-start.2 = (f32[256,384]{0,1:T(8,128)S(1)}, f32[256,384]{0,1:T(8,128)S(1)}, u32[]{:S(2)}, u32[]{:S(2)}) collective-permute-start(f32[256,384]{0,1:T(8,128)S(1)} %bitcast_add_fusion), channel_id=1, source_target_pairs={{0,2},{1,3},{2,0},{3,1},{4,6},{5,7},{6,4},{7,5},{8,10},{9,11},{10,... | collective-permute-start | bytes 1179656 | tf_op jit(solution)/shard_map/ppermute | solution.py:163
  168.2 5.0 %collective-permute-start.3 = (f32[256,128]{0,1:T(8,128)S(1)}, f32[256,128]{0,1:T(8,128)S(1)}, u32[]{:S(2)}, u32[]{:S(2)}) collective-permute-start(f32[256,128]{0,1:T(8,128)S(1)} %slice.54), channel_id=1, source_target_pairs={{0,4},{4,0},{8,12},{12,8},{1,5},{5,1},{9,13},{13,9},{2,6},{6,2},{1... | collective-permute-start | bytes 393224 | tf_op jit(solution)/shard_map/ppermute | solution.py:163
  173.3 16.2 %collective-permute-start.4 = (f32[256,128]{0,1:T(8,128)S(1)}, f32[256,128]{0,1:T(8,128)S(1)}, u32[]{:S(2)}, u32[]{:S(2)}) collective-permute-start(f32[256,128]{0,1:T(8,128)S(1)} %slice_add_fusion.4), channel_id=1, source_target_pairs={{0,8},{4,12},{8,0},{12,4},{1,9},{5,13},{9,1},{13,5},{2,10},{6,14},... | collective-permute-start | bytes 393224 | tf_op jit(solution)/shard_map/ppermute | solution.py:163
  174.4 3.4 %copy-start = (bf16[1024,4096]{1,0:T(8,128)(2,1)S(1)}, bf16[1024,4096]{1,0:T(8,128)(2,1)}, u32[]{:S(2)}) copy-start(bf16[1024,4096]{1,0:T(8,128)(2,1)} %get-tuple-element.6.right_ref) | copy-start | bytes 25165828
  177.7 3.4 %copy-start.3 = (bf16[1024,4096]{1,0:T(8,128)(2,1)S(1)}, bf16[1024,4096]{1,0:T(8,128)(2,1)}, u32[]{:S(2)}) copy-start(bf16[1024,4096]{1,0:T(8,128)(2,1)} %get-tuple-element.5.left_ref) | copy-start | bytes 25165828
  189.8 8.4 %collective-permute-start.5 = (f32[256,128]{1,0:T(8,128)S(1)}, f32[256,128]{1,0:T(8,128)S(1)}, u32[]{:S(2)}, u32[]{:S(2)}) collective-permute-start(f32[256,128]{1,0:T(8,128)S(1)} %fusion.24), channel_id=1, source_target_pairs={{0,1},{1,0},{2,3},{3,2},{4,5},{5,4},{6,7},{7,6},{8,9},{9,8},{10,11... | collective-permute-start | bytes 393224 | tf_op jit(solution)/shard_map/ppermute | solution.py:163
  198.2 9.3 %collective-permute-start.6 = (f32[256,128]{1,0:T(8,128)S(1)}, f32[256,128]{1,0:T(8,128)S(1)}, u32[]{:S(2)}, u32[]{:S(2)}) collective-permute-start(f32[256,128]{1,0:T(8,128)S(1)} %add.127), channel_id=1, source_target_pairs={{0,2},{1,3},{2,0},{3,1},{4,6},{5,7},{6,4},{7,5},{8,10},{9,11},{10,... | collective-permute-start | bytes 393224 | tf_op jit(solution)/shard_map/ppermute | solution.py:163
  207.6 19.5 %collective-permute-start.7 = (f32[256,128]{1,0:T(8,128)S(1)}, f32[256,128]{1,0:T(8,128)S(1)}, u32[]{:S(2)}, u32[]{:S(2)}) collective-permute-start(f32[256,128]{1,0:T(8,128)S(1)} %get-tuple-element.11), channel_id=1, source_target_pairs={{0,4},{4,0},{8,12},{12,8},{1,5},{5,1},{9,13},{13,9},{2,6},{6,2},{1... | collective-permute-start | bytes 393224 | tf_op jit(solution)/shard_map/ppermute | solution.py:163
  209.7 3.4 %copy-start.1 = (bf16[1024,4096]{1,0:T(8,128)(2,1)S(1)}, bf16[1024,4096]{1,0:T(8,128)(2,1)}, u32[]{:S(2)}) copy-start(bf16[1024,4096]{1,0:T(8,128)(2,1)} %get-tuple-element.6.right_ref) | copy-start | bytes 25165828
  213.1 3.4 %copy-start.4 = (bf16[1024,4096]{1,0:T(8,128)(2,1)S(1)}, bf16[1024,4096]{1,0:T(8,128)(2,1)}, u32[]{:S(2)}) copy-start(bf16[1024,4096]{1,0:T(8,128)(2,1)} %get-tuple-element.5.left_ref) | copy-start | bytes 25165828
  224.8 11.7 %collective-permute-start.8 = (f32[256,128]{1,0:T(8,128)S(1)}, f32[256,128]{1,0:T(8,128)S(1)}, u32[]{:S(2)}, u32[]{:S(2)}) collective-permute-start(f32[256,128]{1,0:T(8,128)S(1)} %get-tuple-element.11), channel_id=1, source_target_pairs={{0,8},{4,12},{8,0},{12,4},{1,9},{5,13},{9,1},{13,5},{2,10},{6,14},... | collective-permute-start | bytes 393224 | tf_op jit(solution)/shard_map/ppermute | solution.py:163
  224.8 11.7 %collective-permute-start.9 = (f32[256,128]{1,0:T(8,128)S(1)}, f32[256,128]{1,0:T(8,128)S(1)}, u32[]{:S(2)}, u32[]{:S(2)}) collective-permute-start(f32[256,128]{1,0:T(8,128)S(1)} %get-tuple-element.11), channel_id=1, source_target_pairs={{0,12},{4,8},{8,4},{12,0},{1,13},{5,9},{9,5},{13,1},{2,14},{6,10},... | collective-permute-start | bytes 393224 | tf_op jit(solution)/shard_map/ppermute | solution.py:163
  236.5 15.5 %copy-start.6 = (f32[4,256,128]{2,1,0:T(8,128)}, f32[4,256,128]{2,1,0:T(8,128)S(1)}, u32[]{:S(2)}) copy-start(f32[4,256,128]{2,1,0:T(8,128)S(1)} %bitcast_dynamic-update-slice_fusion) | copy-start | bytes 1572868
  236.9 15.1 %collective-permute-start.10 = (f32[256,128]{1,0:T(8,128)S(1)}, f32[256,128]{1,0:T(8,128)S(1)}, u32[]{:S(2)}, u32[]{:S(2)}) collective-permute-start(f32[256,128]{1,0:T(8,128)S(1)} %fusion.23), channel_id=1, source_target_pairs={{0,1},{1,0},{2,3},{3,2},{4,5},{5,4},{6,7},{7,6},{8,9},{9,8},{10,11... | collective-permute-start | bytes 393224 | tf_op jit(solution)/shard_map/ppermute | solution.py:163
  236.9 3.4 %copy-start.2 = (bf16[1024,4096]{1,0:T(8,128)(2,1)S(1)}, bf16[1024,4096]{1,0:T(8,128)(2,1)}, u32[]{:S(2)}) copy-start(bf16[1024,4096]{1,0:T(8,128)(2,1)} %get-tuple-element.6.right_ref) | copy-start | bytes 25165828
  240.3 3.4 %copy-start.5 = (bf16[1024,4096]{1,0:T(8,128)(2,1)S(1)}, bf16[1024,4096]{1,0:T(8,128)(2,1)}, u32[]{:S(2)}) copy-start(bf16[1024,4096]{1,0:T(8,128)(2,1)} %get-tuple-element.5.left_ref) | copy-start | bytes 25165828
  252.0 9.4 %collective-permute-start.11 = (f32[256,128]{1,0:T(8,128)S(1)}, f32[256,128]{1,0:T(8,128)S(1)}, u32[]{:S(2)}, u32[]{:S(2)}) collective-permute-start(f32[256,128]{1,0:T(8,128)S(1)} %add.136), channel_id=1, source_target_pairs={{0,2},{1,3},{2,0},{3,1},{4,6},{5,7},{6,4},{7,5},{8,10},{9,11},{10,... | collective-permute-start | bytes 393224 | tf_op jit(solution)/shard_map/ppermute | solution.py:163
  261.9 11.6 %collective-permute-start.12 = (f32[128,128]{0,1:T(8,128)S(1)}, f32[128,128]{0,1:T(8,128)S(1)}, u32[]{:S(2)}, u32[]{:S(2)}) collective-permute-start(f32[128,128]{0,1:T(8,128)S(1)} %convolution_multiply_fusion), channel_id=1, source_target_pairs={{0,4},{4,0},{8,12},{12,8},{1,5},{5,1},{9,13},{13,9},{2,6},{6,2},{1... | collective-permute-start | bytes 196616 | tf_op jit(solution)/shard_map/ppermute | solution.py:163
  273.5 31.4 %copy-start.7 = (f32[4,256,128]{2,1,0:T(8,128)S(1)}, f32[4,256,128]{2,1,0:T(8,128)}, u32[]{:S(2)}) copy-start(f32[4,256,128]{2,1,0:T(8,128)} %copy-done.6) | copy-start | bytes 1572868
  273.5 8.4 %collective-permute-start.13 = (f32[128,128]{0,1:T(8,128)S(1)}, f32[128,128]{0,1:T(8,128)S(1)}, u32[]{:S(2)}, u32[]{:S(2)}) collective-permute-start(f32[128,128]{0,1:T(8,128)S(1)} %add.138), channel_id=1, source_target_pairs={{0,8},{4,12},{8,0},{12,4},{1,9},{5,13},{9,1},{13,5},{2,10},{6,14},... | collective-permute-start | bytes 196616 | tf_op jit(solution)/shard_map/ppermute | solution.py:163
